TPU v7x, 32 devices: a whole 2x2x4 slice. The times are simulated.
32 devices in a mesh: feat: 8 (over z, y), cls: 4 (over x, core).
Axes of the slice: x: 2, y: 2, z: 4, core: 2. Of those that a mesh axis runs over, the one named last changes fastest.
Arguments:
- inputs: bfloat16 [2, 1024, 360], P(None, 'feat'), may hold values from -6 to 6
- projection: bfloat16 [360, 65536], P(None, 'feat'), may hold values from -0.3125 to 0.3125
- offsets: int32 [65536], P('feat'), may hold values from 0 to 65520
- labels: int32 [2, 1024], replicated, may hold values from 0 to 4999
- weights: float32 [65536, 5000], P('feat', 'cls'), may hold values from -6 to 6
Outputs:
- updated_weights: float32 [65536, 5000], P('feat', 'cls')
- losses: float32 [2], replicated
All inputs are finite; a program needn't handle non-finite values.
Results may differ from a plain program's by a relative error of at most 0.00061.
Values may be sent and summed in bfloat16 or wider, within the bound.
No kernel may reach another device: no remote copies, remote signals or barrier semaphores. Data moves between devices by JAX's collectives and lax.ppermute only.
A program may use at most 192 MiB of HBM per device.

v0:
```python
import math

import jax
import jax.numpy as jnp
from jax import lax
from jax.sharding import PartitionSpec as P

NFEAT = 65536
NCLS = 5000
PANELS = 2


learning_rate = 10.0


def per_device(inputs, projection, offsets, labels, weights):
    phase = offsets.astype(jnp.float32) * (2.0 * math.pi / 65521.0) - math.pi
    class_count = weights.shape[1]
    first_class = lax.axis_index("cls") * class_count
    classes = jnp.arange(class_count, dtype=jnp.int32) + first_class
    feature_scale = math.sqrt(2.0 / NFEAT)
    losses = []
    for panel_index in range(PANELS):
        angles = (
            jnp.dot(
                lax.all_gather(inputs[panel_index], "feat", axis=0, tiled=True),
                projection,
                preferred_element_type=jnp.float32,
            )
            + phase
        )
        features = (feature_scale * jnp.cos(angles)).astype(jnp.bfloat16)
        narrow = weights.astype(jnp.bfloat16)
        panel_labels = labels[panel_index]
        scores = lax.psum(jnp.dot(features, narrow, preferred_element_type=jnp.float32), "feat")
        is_target = panel_labels[:, None] == classes[None, :]
        target = lax.psum(jnp.sum(jnp.where(is_target, scores, 0.0), axis=1), "cls")
        margin = jnp.where(is_target, 0.0, jnp.maximum(0.0, 1.0 + scores - target[:, None]))
        slope = 2.0 * margin / (NCLS - 1)
        others, row_loss = lax.psum(
            (jnp.sum(slope, axis=1), jnp.sum(margin * margin, axis=1) / (NCLS - 1)), "cls"
        )
        step_grad = jnp.where(is_target, -others[:, None], slope).astype(jnp.bfloat16)
        gradient = lax.dot_general(
            features, step_grad, (((0,), (0,)), ((), ())), preferred_element_type=jnp.float32
        )
        loss = jnp.sum(row_loss)
        weights = weights - learning_rate * gradient
        losses.append(loss)
    return (weights, jnp.stack(losses))


def solution(mesh):
    return jax.shard_map(
        per_device,
        mesh=mesh,
        in_specs=(P(None, "feat", None), P(None, "feat"), P("feat"), P(), P("feat", "cls")),
        out_specs=(P("feat", "cls"), P()),
        check_vma=False,
    )
```

profile of v0, /device:TPU:0, one launch (start us, length us, event | category | flops | bytes accessed | tf_op | source)
XLA Modules:
  0.0 722.8 jit_solution(16753930548696276285)
XLA Ops:
  7.2 0.0 all-reduce.4.cloned.1.call-start
  7.2 0.9 fusion.24
  8.2 30.6 %all-gather = bf16[1,1024,360]{1,2,0:T(8,128)(2,1)S(1)} all-gather(bf16[1,128,360]{1,2,0:T(8,128)(2,1)S(1)} %get-tuple-element.10), channel_id=2, replica_groups=mesh['feat'=8,'cls'=4] {'feat'}, dimensions={1}, use_global_device_ids=true | all-gather | bytes 829440 | tf_op jit(solution)/shard_map/all_gather | solution.py:26
  38.8 0.8 multiply_add_fusion
  39.6 119.2 %multiply_convert_fusion.1 = bf16[1024,8192]{1,0:T(8,128)(2,1)} fusion(bf16[360,8192]{1,0:T(8,128)(2,1)} %param.6, f32[8192]{0:T(1024)S(1)} %multiply_add_fusion, bf16[1,1024,360]{1,2,0:T(8,128)(2,1)S(1)} %all-gather), kind=kOutput, calls=%fused_computation.5 | convolution fusion | flops 6064963584 | bytes 23445504 | tf_op jit(solution)/shard_map/dot_general | solution.py:25
  158.8 29.8 %fusion.4 = f32[1024,1250]{0,1:T(8,128)} fusion(bf16[1024,8192]{1,0:T(8,128)(2,1)} %multiply_convert_fusion.1, f32[8192,1250]{0,1:T(8,128)} %param.9), kind=kOutput, calls=%fused_computation.8 | convolution fusion | flops 20981760000 | bytes 62857216 | tf_op jit(solution)/shard_map/dot_general | solution.py:35
  188.6 0.0 copy-start
  188.6 0.0 all-reduce.4.cloned.1.call-update
  188.6 0.0 all-reduce.6.cloned.1.call-start
  188.7 0.6 copy-done
  189.3 39.0 %all-gather.1 = bf16[1,1024,360]{1,2,0:T(8,128)(2,1)S(1)} all-gather(bf16[1,128,360]{1,2,0:T(8,128)(2,1)S(1)} %get-tuple-element.9), channel_id=3, replica_groups=mesh['feat'=8,'cls'=4] {'feat'}, dimensions={1}, use_global_device_ids=true | all-gather | bytes 829440 | tf_op jit(solution)/shard_map/all_gather | solution.py:26
  228.3 119.2 %multiply_convert_fusion = bf16[1024,8192]{1,0:T(8,128)(2,1)} fusion(bf16[360,8192]{1,0:T(8,128)(2,1)} %param.6, f32[8192]{0:T(1024)S(1)} %multiply_add_fusion, bf16[1,1024,360]{1,2,0:T(8,128)(2,1)S(1)} %all-gather.1), kind=kOutput, calls=%fused_computation.4 | convolution fusion | flops 6064963584 | bytes 23445504 | tf_op jit(solution)/shard_map/dot_general | solution.py:25
  347.5 32.0 %all-reduce.4.cloned.1.call-done = f32[1024,1250]{0,1:T(8,128)} async-done(((f32[1024,1250]{0,1:T(8,128)}), f32[1024,1250]{0,1:T(8,128)}) %all-reduce.4.cloned.1.call-update) | async-done | bytes 5120016 | tf_op jit(solution)/shard_map/psum | solution.py:35
  379.5 3.0 fusion.6
  382.5 6.8 psum.57
  389.4 3.6 multiply_reduce_fusion.1
  392.9 6.0 psum.58
  398.9 40.3 %fusion = f32[8192,1250]{0,1:T(8,128)} fusion(f32[8192,1250]{0,1:T(8,128)} %param.9, bf16[1024,8192]{1,0:T(8,128)(2,1)} %multiply_convert_fusion.1, bf16[1024]{0:T(1024)(128)(2,1)S(1)} %neg.8, s32[1024]{0:T(1024)S(1)} %bitcast.21, s32[1250]{0:T(1024)S(1)} %iota_add_fusion, f32[1024,1250]{0,1:T(8,128)} %all-reduce.4.cloned.1.call-done, f32[1024]{0:T(1024)S(1)} %psum.57), kind=kOutput, calls=%fused_computation.2 | convolution fusion | flops 21000960000 | bytes 103832456 | tf_op jit(solution)/shard_map/dot_general | solution.py:44
  439.2 29.8 %fusion.2 = f32[1024,1250]{0,1:T(8,128)} fusion(bf16[1024,8192]{1,0:T(8,128)(2,1)} %multiply_convert_fusion, f32[8192,1250]{0,1:T(8,128)} %fusion), kind=kOutput, calls=%fused_computation.6 | convolution fusion | flops 20981760000 | bytes 62857216 | tf_op jit(solution)/shard_map/dot_general | solution.py:35
  469.0 0.0 all-reduce.6.cloned.1.call-update
  469.0 179.8 %all-reduce.6.cloned.1.call-done = f32[1024,1250]{0,1:T(8,128)} async-done(((f32[1024,1250]{0,1:T(8,128)}), f32[1024,1250]{0,1:T(8,128)}) %all-reduce.6.cloned.1.call-update) | async-done | bytes 5120016 | tf_op jit(solution)/shard_map/psum | solution.py:35
  648.8 3.0 fusion.8
  651.8 6.8 psum.60
  658.6 3.6 multiply_reduce_fusion
  662.2 10.2 %all-reduce = (f32[1024]{0:T(1024)S(1)}, f32[1024]{0:T(1024)S(1)}, f32[1024]{0:T(1024)S(1)}) all-reduce(f32[1024]{0:T(1024)S(1)} %get-tuple-element.5, f32[1024]{0:T(1024)S(1)} %broadcast_multiply_fusion, f32[1024]{0:T(1024)S(1)} %broadcast_multiply_fusion.1), channel_id=1, replica_groups=mesh['feat'=8,'cls'=4] {'cls'}, use_global_device_ids=true, to_apply=%region_9.10 | all-reduce | flops 3072 | bytes 24576 | tf_op jit(solution)/shard_map/psum | solution.py:40
  672.4 0.7 reduce_sum.77
  673.1 0.6 reduce_sum.79
  673.7 1.9 pad_maximum_fusion
  675.6 40.3 %fusion.1 = f32[8192,1250]{0,1:T(8,128)} fusion(f32[8192,1250]{0,1:T(8,128)} %fusion, bf16[1024,8192]{1,0:T(8,128)(2,1)} %multiply_convert_fusion, bf16[1024]{0:T(1024)(128)(2,1)S(1)} %neg.9, s32[1024]{0:T(1024)S(1)} %bitcast.18, s32[1250]{0:T(1024)S(1)} %iota_add_fusion, f32[1024,1250]{0,1:T(8,128)} %all-reduce.6.cloned.1.call-done, f32[1024]{0:T(1024)S(1)} %psum.60), kind=kOutput, calls=%fused_computation.3 | convolution fusion | flops 21000960000 | bytes 103832456 | tf_op jit(solution)/shard_map/dot_general | solution.py:44
  (6 shorter events, 0.0 us)
Async XLA Ops:
  7.2 372.3 %all-reduce.4.cloned.1.call-start = ((), (), s32[]{:S(2)}) async-start(), calls=%async_computation | async-start | bytes 10289152 | tf_op jit(solution)/shard_map/psum | solution.py:35
  188.6 0.7 copy-start
  188.6 460.1 %all-reduce.6.cloned.1.call-start = ((), (), s32[]{:S(2)}) async-start(), calls=%async_computation.1 | async-start | bytes 10289152 | tf_op jit(solution)/shard_map/psum | solution.py:35
Sparse Core Ops, SparseCore 0:
  188.7 190.7 all-reduce.3
  469.1 179.6 all-reduce.5
where the time goes:
time: 723 us
  matrix products  379 us (52%)
  waiting for transfers between devices  212 us (29%)
  blocking collectives  99.5 us (14%)
  other arithmetic  17.1 us (2%)
  between operations  14.1 us (2%)
    dot_general x2, matrix products, per_device(): jnp.dot(lax.all_gather(inputs[panel_index], 'feat', axis=0, tiled=True),...  238 us
    psum x2, waiting for transfers between devices, per_device(): lax.psum(jnp.dot(features, narrow, preferred_element_type=jnp.float32), '...  212 us
    dot_general x2, matrix products, per_device(): lax.dot_general(features, step_grad, (((0,), (0,)), ((), ())), preferred_...  80.6 us
    all_gather x2, blocking collectives, per_device(): lax.all_gather(inputs[panel_index], 'feat', axis=0, tiled=True)  69.6 us
    dot_general x2, matrix products, per_device(): jnp.dot(features, narrow, preferred_element_type=jnp.float32)  59.6 us
    psum x2, blocking collectives, per_device(): lax.psum((jnp.sum(slope, axis=1), jnp.sum(margin * margin, axis=1) / (NCL...  16.2 us
  transfers between devices with their start and end apart: 2, of which 2 were waited for; matrix products, arithmetic and copies ran while one was open for 16% of the time, Pallas kernels for 0%

commit v1 on v0

v1 whole, which is shorter than its diff:
```python
import functools
import math

import jax
import jax.numpy as jnp
from jax import lax
from jax.experimental import pallas as pl
from jax.experimental.pallas import tpu as pltpu
from jax.sharding import PartitionSpec as P

f32, bf16 = jnp.float32, jnp.bfloat16
learning_rate = 10.0
VMEM_LIMIT = 60 * 1024 * 1024
S0, S1, S2, S3 = 6.283164044274001, -41.33714236744706, 81.34076877058536, -70.99343220053879
NT = (((1,), (1,)), ((), ()))


def features_of(x, p, turns, scale):
    u = jnp.dot(x, p, preferred_element_type=f32) * (0.5 / math.pi) + turns
    t = jnp.abs(u - jnp.round(u)) - 0.25
    s = t * t
    return (t * (scale * S0 + s * (scale * S1 + s * (scale * S2 + s * (scale * S3))))).astype(bf16)


def first_kernel(fb, steps, scale, extra, *refs):
    where_ref, refs = refs[0], refs[1:]
    blocks, refs = refs[:8], refs[8:]
    p_ref, off_ref, w_ref = refs[:3]
    refs = refs[3:]
    if extra:
        e_ref, refs = refs[0], refs[1:]
    f_ref, send_ref, keep_ref, x_ref, now_ref, acc_ref = refs
    j = pl.program_id(0)
    fi, y = where_ref[0], where_ref[1]
    fr = x_ref.shape[0] // 8

    @pl.when(j == 0)
    def _():
        for k in range(8):
            at = pl.multiple_of((fi ^ k) * fr, fr)
            x_ref[pl.ds(at, fr), :] = blocks[k][...].T

    def features(g, slot):
        rows = pl.ds(g * 256, 256)
        turns = off_ref[...].astype(f32) * (1.0 / 65521.0)
        value = features_of(x_ref[rows, :], p_ref[...], turns, scale)
        f_ref[rows, :] = value
        now_ref[slot, rows, :] = value

    def scores(g, slot, start):
        rows = pl.ds(g * 256, 256)
        w = w_ref[...].astype(bf16)
        if extra:
            w = jnp.concatenate([w, e_ref[...]], axis=0)
        s = lax.dot_general(w, now_ref[slot, rows, :], NT, preferred_element_type=f32)
        if start is None:
            acc_ref[g] = s
        else:
            acc_ref[g] += s

    @pl.when(j == 0)
    def _():
        for g in range(4):
            features(g, 0)
            acc_ref[g] = jnp.zeros(acc_ref.shape[1:], f32)

    @pl.when((j > 0) & (j < steps))
    def _():
        for g in range(4):
            features(g, lax.rem(j, 2))
            scores(g, lax.rem(j + 1, 2), 0)

    @pl.when(j == steps)
    def _():
        for g in range(4):
            scores(g, (steps + 1) % 2, 0)
            low, high = acc_ref[g, :, :fr], acc_ref[g, :, fr:]
            send_ref[g] = jnp.where(y == 0, high, low).astype(bf16)
            keep_ref[g] = jnp.where(y == 0, low, high)


def first_call(where, blocks, projection, offsets, wt, extra, rows, scale, fb=512):
    din, nf = projection.shape
    fr = blocks[0].shape[1]
    frames, steps = 8 * fr, nf // fb
    total = rows + (extra.shape[0] // 4 if extra is not None else 0)
    now = lambda j, w: (0, jnp.minimum(j, steps - 1))
    last = lambda j, w: (0, jnp.maximum(j - 1, 0))
    in_specs = [pl.BlockSpec((din, fr), lambda j, w: (0, 0))] * 8 + [
        pl.BlockSpec((din, fb), now),
        pl.BlockSpec((1, fb), now),
        pl.BlockSpec((rows, fb), last),
    ]
    operands = [where, *blocks, projection, offsets, wt]
    if extra is not None:
        in_specs.append(pl.BlockSpec((extra.shape[0] // 4, fb), lambda j, w: (w[2], jnp.maximum(j - 1, 0))))
        operands.append(extra)
    return pl.pallas_call(
        functools.partial(first_kernel, fb, steps, scale, extra is not None),
        grid_spec=pltpu.PrefetchScalarGridSpec(
            num_scalar_prefetch=1,
            grid=(steps + 1,),
            in_specs=in_specs,
            out_specs=[
                pl.BlockSpec((frames, fb), now),
                pl.BlockSpec((4, total, fr), lambda j, w: (0, 0, 0)),
                pl.BlockSpec((4, total, fr), lambda j, w: (0, 0, 0)),
            ],
            scratch_shapes=[
                pltpu.VMEM((frames, din), bf16),
                pltpu.VMEM((2, frames, fb), bf16),
                pltpu.VMEM((4, total, 2 * fr), f32),
            ],
        ),
        out_shape=[
            jax.ShapeDtypeStruct((frames, nf), bf16),
            jax.ShapeDtypeStruct((4, total, fr), bf16),
            jax.ShapeDtypeStruct((4, total, fr), f32),
        ],
        compiler_params=pltpu.CompilerParams(vmem_limit_bytes=VMEM_LIMIT),
        cost_estimate=pl.CostEstimate(
            flops=2 * frames * nf * (din + total), bytes_accessed=nf * (4 * rows + 4 * frames), transcendentals=0
        ),
        name="features_scores",
    )(*operands)


def second_kernel(steps, where_ref, f_ref, w_ref, send_ref, keep_ref, acc_ref):
    j = pl.program_id(0)
    y = where_ref[1]
    fr = send_ref.shape[2]

    @pl.when(j == 0)
    def _():
        acc_ref[...] = jnp.zeros(acc_ref.shape, f32)

    w = w_ref[...].astype(bf16)
    for g in range(4):
        acc_ref[g] += lax.dot_general(w, f_ref[g * 256 : g * 256 + 256, :], NT, preferred_element_type=f32)

    @pl.when(j == steps - 1)
    def _():
        for g in range(4):
            low, high = acc_ref[g, :, :fr], acc_ref[g, :, fr:]
            send_ref[g] = jnp.where(y == 0, high, low).astype(bf16)
            keep_ref[g] = jnp.where(y == 0, low, high)


def second_call(where, features, wt, rows, fb=1024):
    frames, nf = features.shape
    fr, steps = frames // 8, nf // fb
    return pl.pallas_call(
        functools.partial(second_kernel, steps),
        grid_spec=pltpu.PrefetchScalarGridSpec(
            num_scalar_prefetch=1,
            grid=(steps,),
            in_specs=[
                pl.BlockSpec((frames, fb), lambda j, w: (0, j)),
                pl.BlockSpec((rows, fb), lambda j, w: (1, j)),
            ],
            out_specs=[pl.BlockSpec((4, rows, fr), lambda j, w: (0, 0, 0))] * 2,
            scratch_shapes=[pltpu.VMEM((4, rows, 2 * fr), f32)],
        ),
        out_shape=[
            jax.ShapeDtypeStruct((4, rows, fr), bf16),
            jax.ShapeDtypeStruct((4, rows, fr), f32),
        ],
        compiler_params=pltpu.CompilerParams(vmem_limit_bytes=VMEM_LIMIT),
        cost_estimate=pl.CostEstimate(
            flops=2 * frames * nf * rows, bytes_accessed=nf * (4 * rows + 2 * frames), transcendentals=0
        ),
        name="scores",
    )(where, features, wt)


def whole(shape):
    return pl.BlockSpec(shape, lambda *a: (0,) * len(shape))


def small_call(kernel, where, operands, outs, name, scratch=()):
    return pl.pallas_call(
        kernel,
        grid_spec=pltpu.PrefetchScalarGridSpec(
            num_scalar_prefetch=1,
            grid=(1,),
            in_specs=[whole(o.shape) for o in operands],
            out_specs=[whole(s) for s, _ in outs],
            scratch_shapes=list(scratch),
        ),
        out_shape=[jax.ShapeDtypeStruct(s, d) for s, d in outs],
        compiler_params=pltpu.CompilerParams(vmem_limit_bytes=VMEM_LIMIT),
        name=name,
    )(where, *operands)


def add_kernel(where_ref, keep_ref, got_ref, own_ref, a_ref, b_ref, c_ref):
    z = where_ref[3]
    own_ref[...] = keep_ref[z] + got_ref[z].astype(f32)
    for k, out in ((1, a_ref), (2, b_ref), (3, c_ref)):
        out[...] = (keep_ref[z ^ k] + got_ref[z ^ k].astype(f32)).astype(bf16)


def scatter_pair(send):
    return lax.ppermute(send, "feat", [(i, i ^ 1) for i in range(8)])


def scatter_line(where, keep, got):
    shape = keep.shape[1:]
    own, *rest = small_call(add_kernel, where, [keep, got], [(shape, f32)] + [(shape, bf16)] * 3, "pair_sum")
    got = [lax.ppermute(r, "feat", [(i, i ^ (2 * k)) for i in range(8)]) for k, r in zip((1, 2, 3), rest)]
    return [own, *got]


def over_cls(x):
    return [x] + [lax.ppermute(x, "cls", [(i, i ^ k) for i in range(4)]) for k in (1, 2, 3)]


def total(parts):
    return (parts[0] + parts[1].astype(f32)) + (parts[2].astype(f32) + parts[3].astype(f32))


def gram_kernel(where_ref, *refs):
    parts, out = refs[:4], refs[4]
    out[...] = total([p[pl.ds(p.shape[0] - out.shape[0], out.shape[0]), :] for p in parts])


def target_kernel(rows, count, steps_of, where_ref, *refs):
    first, second, refs = refs[:4], refs[4:8], refs[8:]
    lab_ref, refs = refs[0], refs[1:]
    if steps_of:
        gram, ga, gb, refs = refs[:4], refs[4:12], refs[12:20], refs[20:]
    s_ref, t_ref, refs = refs[0], refs[1], refs[2:]
    fr = s_ref.shape[1]
    s_ref[0:rows, :] = total([r[0:rows, :] for r in first])
    s_ref[rows : 2 * rows, :] = total([r[...] for r in second])
    if steps_of:
        fi, q = where_ref[0], where_ref[2]
        hi_ref, lo_ref = refs
        quarter = gram[0].shape[0]
        for k in range(4):
            at = pl.ds(pl.multiple_of((q ^ k) * quarter, quarter), quarter)
            value = gram[k][...]
            hi = value.astype(bf16)
            hi_ref[at, :] = hi
            lo_ref[at, :] = (value - hi.astype(f32)).astype(bf16)
        for r, g in ((0, ga), (rows, gb)):
            change = jnp.zeros((rows, fr), f32)
            for k in range(8):
                at = pl.ds(pl.multiple_of((fi ^ k) * fr, fr), fr)
                change += jnp.dot(g[k][...], hi_ref[at, :], preferred_element_type=f32)
                change += jnp.dot(g[k][...], lo_ref[at, :], preferred_element_type=f32)
            s_ref[r : r + rows, :] -= learning_rate * change
    row = lax.broadcasted_iota(jnp.int32, s_ref.shape, 0)
    is_target = (row + where_ref[2] * count == lab_ref[...]) & (row < count)
    t_ref[...] = jnp.sum(jnp.where(is_target, s_ref[...], 0.0), axis=0, keepdims=True)


def margin_kernel(count, classes, where_ref, s_ref, lab_ref, t0, t1, t2, t3, slope_ref, sums_ref):
    target = (t0[...] + t1[...]) + (t2[...] + t3[...])
    row = lax.broadcasted_iota(jnp.int32, s_ref.shape, 0)
    valid = row < count
    is_target = row + where_ref[2] * count == lab_ref[...]
    margin = jnp.where(valid & ~is_target, jnp.maximum(0.0, 1.0 + s_ref[...] - target), 0.0)
    slope = 2.0 * margin / (classes - 1)
    slope_ref[...] = slope
    sums_ref[0:1, :] = jnp.sum(slope, axis=0, keepdims=True)
    sums_ref[1:2, :] = jnp.sum(margin * margin, axis=0, keepdims=True) / (classes - 1)


def grad_kernel(rows, count, where_ref, slope_ref, lab_ref, s0, s1, s2, s3, a_ref, b_ref, loss_ref):
    sums = (s0[...] + s1[...]) + (s2[...] + s3[...])
    row = lax.broadcasted_iota(jnp.int32, slope_ref.shape, 0)
    is_target = (row + where_ref[2] * count == lab_ref[...]) & (row < count)
    value = jnp.where(is_target, -sums[0:1, :], slope_ref[...]).astype(bf16)
    a_ref[...] = value[:rows]
    b_ref[...] = value[rows:]
    loss_ref[...] = sums[1:2, :]


def spread(block):
    line = [block] + [lax.ppermute(block, "feat", [(i, i ^ (2 * k)) for i in range(8)]) for k in (1, 2, 3)]
    out = []
    for b in line:
        out += [b, lax.ppermute(b, "feat", [(i, i ^ 1) for i in range(8)])]
    return out


def update_kernel(parts, where_ref, *refs):
    rows = refs[0].shape[0]
    grads, refs = refs[: 8 * parts], refs[8 * parts :]
    f_ref, w_ref, out_ref, g_ref = refs[0], refs[1], refs[-2], refs[-1]
    fr = grads[0].shape[1]
    fi = where_ref[0]

    @pl.when(pl.program_id(0) == 0)
    def _():
        for part in range(parts):
            for k in range(8):
                at = pl.ds(pl.multiple_of((fi ^ k) * fr, fr), fr)
                g_ref[part * rows : (part + 1) * rows, at] = grads[8 * part + k][...]

    change = jnp.dot(g_ref[...], f_ref[...], preferred_element_type=f32)
    out_ref[...] = w_ref[...] - learning_rate * change[: out_ref.shape[0]]


def update_call(where, grads, features, wt, place, alias, fb=512):
    frames, nf = features.shape
    rows, fr = grads[0].shape
    parts = len(grads) // 8
    block = wt.shape[0] if parts == 2 else rows
    spec = pl.BlockSpec((block, fb), lambda j, w: (place, j))
    return pl.pallas_call(
        functools.partial(update_kernel, parts),
        grid_spec=pltpu.PrefetchScalarGridSpec(
            num_scalar_prefetch=1,
            grid=(nf // fb,),
            in_specs=[whole((rows, fr))] * len(grads) + [pl.BlockSpec((frames, fb), lambda j, w: (0, j)), spec],
            out_specs=spec,
            scratch_shapes=[pltpu.VMEM((parts * rows, frames), bf16)],
        ),
        out_shape=jax.ShapeDtypeStruct(wt.shape, f32),
        input_output_aliases={len(grads) + 2: 0} if alias else {},
        compiler_params=pltpu.CompilerParams(vmem_limit_bytes=VMEM_LIMIT),
        cost_estimate=pl.CostEstimate(
            flops=2 * frames * nf * rows * parts,
            bytes_accessed=nf * (8 * rows * parts + 2 * frames),
            transcendentals=0,
        ),
        name="update",
    )(where, *grads, features, wt)


def per_device(nfeat, ncls, inputs, projection, offsets, labels, weights):
    fi, q = lax.axis_index("feat"), lax.axis_index("cls")
    where = jnp.stack([fi, fi & 1, q, fi >> 1]).astype(jnp.int32)
    scale = math.sqrt(2.0 / nfeat)
    wt = weights.T
    xt = jnp.swapaxes(inputs, 1, 2)
    fr = xt.shape[2]
    count = wt.shape[0]
    rows = -(-count // 256) * 128
    turns = offsets.reshape(1, -1)
    own_labels = lax.dynamic_slice_in_dim(labels, fi * fr, fr, 1)

    x = [
        [xt[p]] + [lax.ppermute(xt[p], "feat", [(i, i ^ k) for i in range(8)]) for k in range(1, 8)] for p in range(2)
    ]

    def step(p, first, second, extra):
        lab = own_labels[p : p + 1]
        shape = (2 * rows, fr)
        scratch = [pltpu.VMEM((8 * fr, fr), bf16)] * 2 if extra else []
        s, t = small_call(
            functools.partial(target_kernel, rows, count, bool(extra)),
            where,
            [*first, *second, lab, *extra],
            [(shape, f32), ((1, fr), f32)],
            "target",
            scratch,
        )
        slope, sums = small_call(
            functools.partial(margin_kernel, count, ncls),
            where,
            [s, lab, *over_cls(t)],
            [(shape, f32), ((2, fr), f32)],
            "margin",
        )
        ga, gb, loss = small_call(
            functools.partial(grad_kernel, rows, count),
            where,
            [slope, lab, *over_cls(sums)],
            [((rows, fr), bf16), ((rows, fr), bf16), ((1, fr), f32)],
            "step_grad",
        )
        return spread(ga), spread(gb), loss

    f1, send1a, keep1a = first_call(where, x[0], projection, turns, wt, None, rows, scale)
    got1a = scatter_pair(send1a)
    send1b, keep1b = second_call(where, f1, wt, rows)
    got1b = scatter_pair(send1b)
    first1 = scatter_line(where, keep1a, got1a)
    second1 = scatter_line(where, keep1b, got1b)
    f2, send2a, keep2a = first_call(where, x[1], projection, turns, wt, f1, rows, scale)
    got2a = scatter_pair(send2a)
    send2b, keep2b = second_call(where, f2, wt, rows)
    got2b = scatter_pair(send2b)
    g1a, g1b, loss1 = step(0, first1, second1, [])
    first2 = scatter_line(where, keep2a, got2a)
    second2 = scatter_line(where, keep2b, got2b)
    (gram,) = small_call(gram_kernel, where, first2, [((8 * fr // 4, fr), f32)], "gram")
    grams = over_cls(gram)
    g2a, g2b, loss2 = step(1, first2, second2, [*grams, *g1a, *g1b])
    w1 = update_call(where, g1a + g1b, f1, wt, 0, False)
    w2 = update_call(where, g2a, f2, w1, 0, True)
    w2 = update_call(where, g2b, f2, w2, 1, True)
    losses = lax.psum(jnp.stack([jnp.sum(loss1), jnp.sum(loss2)]), "feat")
    return w2.T, losses


def plain_device(nfeat, ncls, inputs, projection, offsets, labels, weights):
    phase = offsets.astype(f32) * (2.0 * math.pi / 65521.0) - math.pi
    classes = jnp.arange(weights.shape[1], dtype=jnp.int32) + lax.axis_index("cls") * weights.shape[1]
    losses = []
    for p in range(inputs.shape[0]):
        x = lax.all_gather(inputs[p], "feat", axis=0, tiled=True)
        features = (math.sqrt(2.0 / nfeat) * jnp.cos(jnp.dot(x, projection, preferred_element_type=f32) + phase)).astype(bf16)
        scores = lax.psum(jnp.dot(features, weights.astype(bf16), preferred_element_type=f32), "feat")
        is_target = labels[p][:, None] == classes[None, :]
        target = lax.psum(jnp.sum(jnp.where(is_target, scores, 0.0), axis=1), "cls")
        margin = jnp.where(is_target, 0.0, jnp.maximum(0.0, 1.0 + scores - target[:, None]))
        slope = 2.0 * margin / (ncls - 1)
        others, row_loss = lax.psum((jnp.sum(slope, axis=1), jnp.sum(margin * margin, axis=1) / (ncls - 1)), "cls")
        grad = jnp.where(is_target, -others[:, None], slope).astype(bf16)
        weights = weights - learning_rate * lax.dot_general(features, grad, (((0,), (0,)), ((), ())), preferred_element_type=f32)
        losses.append(jnp.sum(row_loss))
    return weights, jnp.stack(losses)


def solution(mesh):
    kernels = mesh.shape["feat"] == 8 and mesh.shape["cls"] == 4

    def program(inputs, projection, offsets, labels, weights):
        nfeat, ncls = weights.shape
        body = per_device if kernels and inputs.shape[:2] == (2, 1024) else plain_device
        return jax.shard_map(
            functools.partial(body, nfeat, ncls),
            mesh=mesh,
            in_specs=(P(None, "feat", None), P(None, "feat"), P("feat"), P(), P("feat", "cls")),
            out_specs=(P("feat", "cls"), P()),
            check_vma=False,
        )(inputs, projection, offsets, labels, weights)

    return program
```

time: 723 us -> 477 us (0.66)
  matrix products: 379 us -> 0 us
  Pallas kernels: 0 us -> 263 us
  waiting for transfers between devices: 212 us -> 63.6 us
  starting transfers between devices: 0.08 us -> 109 us
  blocking collectives: 99.5 us -> 25.2 us
  between operations: 14.1 us -> 1.27 us
  other arithmetic: 17.1 us -> 4.49 us
  local copies, waits for them, and re-layouts: 1.56 us -> 9.1 us
    dot_general x6 -> x0, matrix products: 379 us -> none  [the longest x2 238 us: per_device(): jnp.dot(lax.all_gather(inputs[panel_index], 'feat', axis=0, tiled=True),...]
    pallas_call x0 -> x18, Pallas kernels: none -> 263 us  [the longest x3 107 us: update_call(): pl.pallas_call(functools.partial(update_kernel, parts), grid_spec=pltpu.P...]
    psum x2 -> x0, waiting for transfers between devices: 212 us -> none  [per_device(): lax.psum(jnp.dot(features, narrow, preferred_element_type=jnp.float32), '...]
    ppermute x0 -> x73, starting transfers between devices: none -> 109 us  [the longest x12 30.5 us: scatter_line(): lax.ppermute(r, 'feat', [(i, i ^ 2 * k) for i in range(8)])]
    all_gather x2 -> x0, blocking collectives: 69.6 us -> none  [per_device(): lax.all_gather(inputs[panel_index], 'feat', axis=0, tiled=True)]
    ppermute x0 -> x73, waiting for transfers between devices: none -> 63.6 us  [the longest x15 19.4 us: over_cls(): lax.ppermute(x, 'cls', [(i, i ^ k) for i in range(4)])]
    reduce_sum x6 -> x2, other arithmetic: 14.5 us -> 2.55 us  [per_device(): losses = lax.psum(jnp.stack([jnp.sum(loss1), jnp.sum(loss2)]), 'feat')]
    psum x4 -> x1, blocking collectives: 29.9 us -> 25.2 us  [per_device(): losses = lax.psum(jnp.stack([jnp.sum(loss1), jnp.sum(loss2)]), 'feat')]
  transfers between devices with their start and end apart: 2 -> 73, of which waited for: 2 -> 22; matrix products, arithmetic and copies ran while one was open for 16% -> 1% of each run, Pallas kernels for 0% -> 47%
where the time goes in v1:
time: 477 us; the launch traced here: 476 us
  Pallas kernels  263 us (55%)
  starting transfers between devices  109 us (23%)
  waiting for transfers between devices  63.6 us (13%)
  blocking collectives  25.2 us (5%)
  local copies, waits for them, and re-layouts  9.1 us (2%)
    pallas_call x3, Pallas kernels, update_call(): pl.pallas_call(functools.partial(update_kernel, parts), grid_spec=pltpu.P...  107 us
    pallas_call x2, Pallas kernels, first_call(): pl.pallas_call(functools.partial(first_kernel, fb, steps, scale, extra is...  80.7 us
    pallas_call x2, Pallas kernels, second_call(): pl.pallas_call(functools.partial(second_kernel, steps), grid_spec=pltpu.P...  40.3 us
    pallas_call x11, Pallas kernels, small_call(): pl.pallas_call(kernel, grid_spec=pltpu.PrefetchScalarGridSpec(num_scalar_...  35.3 us
    ppermute x12, starting transfers between devices, scatter_line(): lax.ppermute(r, 'feat', [(i, i ^ 2 * k) for i in range(8)])  30.5 us
    ppermute x14, starting transfers between devices, per_device(): lax.ppermute(xt[p], 'feat', [(i, i ^ k) for i in range(8)])  26.1 us
    psum x1, blocking collectives, per_device(): losses = lax.psum(jnp.stack([jnp.sum(loss1), jnp.sum(loss2)]), 'feat')  25.2 us
    ppermute x12, starting transfers between devices, spread(): lax.ppermute(block, 'feat', [(i, i ^ 2 * k) for i in range(8)])  20.3 us
  transfers between devices with their start and end apart: 73, of which 22 were waited for; matrix products, arithmetic and copies ran while one was open for 1% of the time, Pallas kernels for 47%

profile of v1, /device:TPU:0, one launch (start us, length us, event | category | flops | bytes accessed | tf_op | source)
XLA Modules:
  0.0 476.0 jit_solution(6491279884075871902)
XLA Ops:
  1.6 4.1 collective-permute-start.10
  7.0 3.6 collective-permute-start.12
  12.3 3.6 collective-permute-done.10.refs_5_
  17.1 3.0 collective-permute-done.11.refs_6_
  21.2 3.7 collective-permute-start.1
  24.9 3.5 collective-permute-start.3
  28.5 2.1 collective-permute-start.4
  30.6 37.9 %features_scores.2 = (bf16[1024,8192]{1,0:T(8,128)(2,1)}, bf16[4,640,128]{2,1,0:T(8,128)(2,1)}, f32[4,640,128]{2,1,0:T(8,128)}) custom-call(s32[4]{0:T(128)} %pad_add_fusion.refs_0_.where_ref, bf16[360,128]{1,0:T(8,128)(2,1)} %copy-done.51, bf16[360,128]{1,0:T(8,128)(2,1)} %copy-done.70, bf16[360,128]{1,0:T(8,128)(2,1)} %copy-done.75, ...), custom_call_target="tpu_custom_call" | custom-call | flops 16777216000 | bytes 54525952 | tf_op jit(solution)/shard_map/features_scores/pallas_call | solution.py:98
  68.5 2.4 collective-permute-start.5
  71.0 2.0 collective-permute-start.6
  73.0 20.1 %scores.3 = (bf16[4,640,128]{2,1,0:T(8,128)(2,1)}, f32[4,640,128]{2,1,0:T(8,128)}) custom-call(s32[4]{0:T(128)} %pad_add_fusion.refs_0_.where_ref, bf16[1024,8192]{1,0:T(8,128)(2,1)} %get-tuple-element.42.refs_12_.f_ref.refs_16_, f32[1250,8192]{1,0:T(8,128)} %bitcast.15), custom_call_target="tpu_custom_call" | custom-call | flops 10737418240 | bytes 37748736 | tf_op jit(solution)/shard_map/scores/pallas_call | solution.py:152
  96.6 42.7 %features_scores.3 = (bf16[1024,8192]{1,0:T(8,128)(2,1)}, bf16[4,896,128]{2,1,0:T(8,128)(2,1)}, f32[4,896,128]{2,1,0:T(8,128)}) custom-call(s32[4]{0:T(128)} %pad_add_fusion.refs_0_.where_ref, bf16[360,128]{1,0:T(8,128)(2,1)} %copy-done.50, bf16[360,128]{1,0:T(8,128)(2,1)} %copy-done.68, bf16[360,128]{1,0:T(8,128)(2,1)} %copy-done.71, ...), custom_call_target="tpu_custom_call" | custom-call | flops 21072183296 | bytes 54525952 | tf_op jit(solution)/shard_map/features_scores/pallas_call | solution.py:98
  139.3 20.2 %scores.2 = (bf16[4,640,128]{2,1,0:T(8,128)(2,1)}, f32[4,640,128]{2,1,0:T(8,128)}) custom-call(s32[4]{0:T(128)} %pad_add_fusion.refs_0_.where_ref, bf16[1024,8192]{1,0:T(8,128)(2,1)} %get-tuple-element.49.f_ref.refs_8_, f32[1250,8192]{1,0:T(8,128)} %bitcast.17), custom_call_target="tpu_custom_call" | custom-call | flops 10737418240 | bytes 37748736 | tf_op jit(solution)/shard_map/scores/pallas_call | solution.py:152
  162.4 3.1 pair_sum.7
  165.5 2.4 collective-permute-start.31
  167.9 2.0 collective-permute-start.32
  169.9 3.1 pair_sum.6
  173.0 4.3 collective-permute-done.18.got_ref
  177.4 2.4 collective-permute-start.27
  179.8 3.1 pair_sum.5
  182.9 2.0 collective-permute-start.28
  185.0 3.0 collective-permute-start.19
  188.4 9.7 %collective-permute-done.27.refs_2_ = bf16[640,128]{1,0:T(8,128)(2,1)S(1)} collective-permute-done((bf16[640,128]{1,0:T(8,128)(2,1)}, bf16[640,128]{1,0:T(8,128)(2,1)S(1)}, u32[]{:S(2)}, u32[]{:S(2)}) %collective-permute-start.27) | collective-permute-done | bytes 163872 | tf_op jit(solution)/shard_map/ppermute | solution.py:210
  198.0 1.9 collective-permute-start.21
  201.1 3.2 target.2
  207.0 2.1 collective-permute-done.34.t2
  209.4 2.9 collective-permute-done.35.t3
  212.8 2.9 margin.2
  218.5 2.3 collective-permute-done.37.s2
  220.8 3.0 collective-permute-done.38.s3
  224.4 2.5 step_grad.2
  229.5 1.9 collective-permute-start.44
  233.9 2.9 collective-permute-done.40.refs_15_.refs_2_
  236.8 2.0 collective-permute-start.51
  238.9 3.5 pair_sum.4
  244.0 11.5 %collective-permute-start.16 = (bf16[896,128]{1,0:T(8,128)(2,1)}, bf16[896,128]{1,0:T(8,128)(2,1)S(1)}, u32[]{:S(2)}, u32[]{:S(2)}) collective-permute-start(bf16[896,128]{1,0:T(8,128)(2,1)} %get-tuple-element.47), channel_id=1, source_target_pairs={{0,16},{4,20},{8,24},{12,28},{16,0},{20,4},{24,8},{28,12},{1,17},{... | collective-permute-start | bytes 688136 | tf_op jit(solution)/shard_map/ppermute | solution.py:210
  255.5 3.1 collective-permute-start.39
  258.6 6.8 %collective-permute-done.49.refs_25_.refs_12_ = bf16[640,128]{1,0:T(8,128)(2,1)S(1)} collective-permute-done((bf16[640,128]{1,0:T(8,128)(2,1)}, bf16[640,128]{1,0:T(8,128)(2,1)S(1)}, u32[]{:S(2)}, u32[]{:S(2)}) %collective-permute-start.49) | collective-permute-done | bytes 163872 | tf_op jit(solution)/shard_map/ppermute | solution.py:281
  265.4 5.0 %collective-permute-start.17 = (bf16[896,128]{1,0:T(8,128)(2,1)}, bf16[896,128]{1,0:T(8,128)(2,1)S(1)}, u32[]{:S(2)}, u32[]{:S(2)}) collective-permute-start(bf16[896,128]{1,0:T(8,128)(2,1)} %get-tuple-element.48), channel_id=1, source_target_pairs={{0,24},{4,28},{8,16},{12,20},{16,8},{20,12},{24,0},{28,4},{1,25},{... | collective-permute-start | bytes 688136 | tf_op jit(solution)/shard_map/ppermute | solution.py:210
  273.0 3.3 collective-permute-done.16.refs_2_
  276.3 2.0 collective-permute-start.48
  278.4 1.9 collective-permute-start.52
  280.3 2.6 gram.1.refs_9_
  283.0 2.1 collective-permute-start.23
  285.1 2.9 collective-permute-done.50.refs_26_.refs_13_
  288.0 1.8 collective-permute-done.52.refs_28_.refs_15_
  292.0 5.7 %target.3 = (f32[1280,128]{1,0:T(8,128)}, f32[1,128]{1,0:T(1,128)}) custom-call(s32[4]{0:T(128)} %pad_add_fusion.refs_0_.where_ref, f32[896,128]{1,0:T(8,128)} %get-tuple-element.45.refs_0_, bf16[896,128]{1,0:T(8,128)(2,1)} %copy-done.3, bf16[896,128]{1,0:T(8,128)(2,1)} %copy-done.4, bf16[896,128]{1,0:T(8,128)(2,1)} %copy-done.5, ...), custom_call_target="tpu_custom_call" | custom-call | tf_op jit(solution)/shard_map/target/pallas_call | solution.py:181
  299.7 2.1 collective-permute-done.54.t2
  303.1 2.9 margin.3
  307.8 1.9 collective-permute-done.57.s2
  310.3 2.5 step_grad.3
  312.9 2.9 collective-permute-start.67
  318.5 2.0 collective-permute-start.66
  325.1 2.2 collective-permute-start.62
  327.3 3.7 collective-permute-done.69.refs_4_
  331.0 2.7 collective-permute-start.64
  333.8 2.0 collective-permute-start.68
  335.8 1.9 collective-permute-start.72
  337.8 46.9 %update.3.refs_9_ = f32[1250,8192]{1,0:T(8,128)} custom-call(s32[4]{0:T(128)} %pad_add_fusion.refs_0_.where_ref, bf16[640,128]{1,0:T(8,128)(2,1)} %get-tuple-element.72.refs_13_.refs_0_, bf16[640,128]{1,0:T(8,128)(2,1)} %copy-done.12, bf16[640,128]{1,0:T(8,128)(2,1)} %copy-done.6, bf16[640,128]{1,0:T(8,128)(2,1)} %copy-done.14, bf16[640,128]{1,0:T(8,128)(2,1)} %copy-done.7, ...), custom_call_target="tpu_custom_call" | custom-call | flops 21474836480 | bytes 100663296 | tf_op jit(solution)/shard_map/update/pallas_call | solution.py:312
  384.7 25.2 %psum.7 = f32[2]{0:T(128)} all-reduce(f32[2]{0:T(128)S(1)} %pad_maximum_fusion), channel_id=1, replica_groups=mesh['feat'=8,'cls'=4] {'feat'}, use_global_device_ids=true, to_apply=%region_2.0 | all-reduce | flops 2 | bytes 16 | tf_op jit(solution)/shard_map/psum | solution.py:396
  409.9 2.1 collective-permute-start.61
  412.1 1.9 collective-permute-start.65
  414.7 30.0 %update.4.refs_9_ = f32[1250,8192]{1,0:T(8,128)} custom-call(s32[4]{0:T(128)} %pad_add_fusion.refs_0_.where_ref, bf16[640,128]{1,0:T(8,128)(2,1)} %get-tuple-element.79.refs_0_, bf16[640,128]{1,0:T(8,128)(2,1)} %copy-done.29, bf16[640,128]{1,0:T(8,128)(2,1)} %copy-done.25, bf16[640,128]{1,0:T(8,128)(2,1)} %copy-done.31, ...), custom_call_target="tpu_custom_call", output_to_operand_aliasing={{}: (10, {})} | custom-call | flops 10737418240 | bytes 58720256 | tf_op jit(solution)/shard_map/update/pallas_call | solution.py:312
  446.2 29.8 %update.5 = f32[1250,8192]{1,0:T(8,128)} custom-call(s32[4]{0:T(128)} %pad_add_fusion.refs_0_.where_ref, bf16[640,128]{1,0:T(8,128)(2,1)} %get-tuple-element.78.refs_0_, bf16[640,128]{1,0:T(8,128)(2,1)} %copy-done.34, bf16[640,128]{1,0:T(8,128)(2,1)} %copy-done.24, bf16[640,128]{1,0:T(8,128)(2,1)} %copy-done.35, ...), custom_call_target="tpu_custom_call", output_to_operand_aliasing={{}: (10, {})} | custom-call | flops 10737418240 | bytes 58720256 | tf_op jit(solution)/shard_map/update/pallas_call | solution.py:312
  (266 shorter events, 48.0 us)
Async XLA Ops:
  1.6 14.2 %collective-permute-start.10 = (bf16[360,128]{1,0:T(8,128)(2,1)S(1)}, bf16[360,128]{1,0:T(8,128)(2,1)S(1)}, u32[]{:S(2)}, u32[]{:S(2)}) collective-permute-start(bf16[360,128]{1,0:T(8,128)(2,1)S(1)} %get-tuple-element.82.refs_1_), channel_id=1, source_target_pairs={{0,16},{4,20},{8,24},{12,28},{16,0},{20,4},{24,8},{28,12},{1,17},{... | collective-permute-start | bytes 276488 | tf_op jit(solution)/shard_map/ppermute | solution.py:346
  5.7 14.4 %collective-permute-start.11 = (bf16[360,128]{1,0:T(8,128)(2,1)S(1)}, bf16[360,128]{1,0:T(8,128)(2,1)S(1)}, u32[]{:S(2)}, u32[]{:S(2)}) collective-permute-start(bf16[360,128]{1,0:T(8,128)(2,1)S(1)} %get-tuple-element.82.refs_1_), channel_id=1, source_target_pairs={{0,20},{4,16},{8,28},{12,24},{16,4},{20,0},{24,12},{28,8},{1,21},{... | collective-permute-start | bytes 276488 | tf_op jit(solution)/shard_map/ppermute | solution.py:346
  7.0 13.9 %collective-permute-start.12 = (bf16[360,128]{1,0:T(8,128)(2,1)S(1)}, bf16[360,128]{1,0:T(8,128)(2,1)S(1)}, u32[]{:S(2)}, u32[]{:S(2)}) collective-permute-start(bf16[360,128]{1,0:T(8,128)(2,1)S(1)} %get-tuple-element.82.refs_1_), channel_id=1, source_target_pairs={{0,24},{4,28},{8,16},{12,20},{16,8},{20,12},{24,0},{28,4},{1,25},{... | collective-permute-start | bytes 276488 | tf_op jit(solution)/shard_map/ppermute | solution.py:346
  10.6 10.6 %collective-permute-start.13 = (bf16[360,128]{1,0:T(8,128)(2,1)S(1)}, bf16[360,128]{1,0:T(8,128)(2,1)S(1)}, u32[]{:S(2)}, u32[]{:S(2)}) collective-permute-start(bf16[360,128]{1,0:T(8,128)(2,1)S(1)} %get-tuple-element.82.refs_1_), channel_id=1, source_target_pairs={{0,28},{4,24},{8,20},{12,16},{16,12},{20,8},{24,4},{28,0},{1,29},{... | collective-permute-start | bytes 276488 | tf_op jit(solution)/shard_map/ppermute | solution.py:346
  10.6 14.3 %collective-permute-start.7 = (bf16[360,128]{1,0:T(8,128)(2,1)S(1)}, bf16[360,128]{1,0:T(8,128)(2,1)S(1)}, u32[]{:S(2)}, u32[]{:S(2)}) collective-permute-start(bf16[360,128]{1,0:T(8,128)(2,1)S(1)} %get-tuple-element.82.refs_1_), channel_id=1, source_target_pairs={{0,4},{4,0},{8,12},{12,8},{16,20},{20,16},{24,28},{28,24},{1,5},{5... | collective-permute-start | bytes 276488 | tf_op jit(solution)/shard_map/ppermute | solution.py:346
  15.9 9.1 %collective-permute-start.8 = (bf16[360,128]{1,0:T(8,128)(2,1)S(1)}, bf16[360,128]{1,0:T(8,128)(2,1)S(1)}, u32[]{:S(2)}, u32[]{:S(2)}) collective-permute-start(bf16[360,128]{1,0:T(8,128)(2,1)S(1)} %get-tuple-element.82.refs_1_), channel_id=1, source_target_pairs={{0,8},{4,12},{8,0},{12,4},{16,24},{20,28},{24,16},{28,20},{1,9},{5... | collective-permute-start | bytes 276488 | tf_op jit(solution)/shard_map/ppermute | solution.py:346
  20.1 8.3 %collective-permute-start.9 = (bf16[360,128]{1,0:T(8,128)(2,1)S(1)}, bf16[360,128]{1,0:T(8,128)(2,1)S(1)}, u32[]{:S(2)}, u32[]{:S(2)}) collective-permute-start(bf16[360,128]{1,0:T(8,128)(2,1)S(1)} %get-tuple-element.82.refs_1_), channel_id=1, source_target_pairs={{0,12},{4,8},{8,4},{12,0},{16,28},{20,24},{24,20},{28,16},{1,13},{... | collective-permute-start | bytes 276488 | tf_op jit(solution)/shard_map/ppermute | solution.py:346
  20.9 47.6 %collective-permute-start = (bf16[360,128]{1,0:T(8,128)(2,1)S(1)}, bf16[360,128]{1,0:T(8,128)(2,1)S(1)}, u32[]{:S(2)}, u32[]{:S(2)}) collective-permute-start(bf16[360,128]{1,0:T(8,128)(2,1)S(1)} %get-tuple-element.83.refs_1_), channel_id=1, source_target_pairs={{0,4},{4,0},{8,12},{12,8},{16,20},{20,16},{24,28},{28,24},{1,5},{5... | collective-permute-start | bytes 276488 | tf_op jit(solution)/shard_map/ppermute | solution.py:346
  21.2 49.8 %collective-permute-start.1 = (bf16[360,128]{1,0:T(8,128)(2,1)S(1)}, bf16[360,128]{1,0:T(8,128)(2,1)S(1)}, u32[]{:S(2)}, u32[]{:S(2)}) collective-permute-start(bf16[360,128]{1,0:T(8,128)(2,1)S(1)} %get-tuple-element.83.refs_1_), channel_id=1, source_target_pairs={{0,8},{4,12},{8,0},{12,4},{16,24},{20,28},{24,16},{28,20},{1,9},{5... | collective-permute-start | bytes 276488 | tf_op jit(solution)/shard_map/ppermute | solution.py:346
  24.9 68.2 %collective-permute-start.2 = (bf16[360,128]{1,0:T(8,128)(2,1)S(1)}, bf16[360,128]{1,0:T(8,128)(2,1)S(1)}, u32[]{:S(2)}, u32[]{:S(2)}) collective-permute-start(bf16[360,128]{1,0:T(8,128)(2,1)S(1)} %get-tuple-element.83.refs_1_), channel_id=1, source_target_pairs={{0,12},{4,8},{8,4},{12,0},{16,28},{20,24},{24,20},{28,16},{1,13},{... | collective-permute-start | bytes 276488 | tf_op jit(solution)/shard_map/ppermute | solution.py:346
  24.9 69.2 %collective-permute-start.3 = (bf16[360,128]{1,0:T(8,128)(2,1)S(1)}, bf16[360,128]{1,0:T(8,128)(2,1)S(1)}, u32[]{:S(2)}, u32[]{:S(2)}) collective-permute-start(bf16[360,128]{1,0:T(8,128)(2,1)S(1)} %get-tuple-element.83.refs_1_), channel_id=1, source_target_pairs={{0,16},{4,20},{8,24},{12,28},{16,0},{20,4},{24,8},{28,12},{1,17},{... | collective-permute-start | bytes 276488 | tf_op jit(solution)/shard_map/ppermute | solution.py:346
  28.5 66.8 %collective-permute-start.4 = (bf16[360,128]{1,0:T(8,128)(2,1)S(1)}, bf16[360,128]{1,0:T(8,128)(2,1)S(1)}, u32[]{:S(2)}, u32[]{:S(2)}) collective-permute-start(bf16[360,128]{1,0:T(8,128)(2,1)S(1)} %get-tuple-element.83.refs_1_), channel_id=1, source_target_pairs={{0,20},{4,16},{8,28},{12,24},{16,4},{20,0},{24,12},{28,8},{1,21},{... | collective-permute-start | bytes 276488 | tf_op jit(solution)/shard_map/ppermute | solution.py:346
  68.5 26.7 %collective-permute-start.5 = (bf16[360,128]{1,0:T(8,128)(2,1)S(1)}, bf16[360,128]{1,0:T(8,128)(2,1)S(1)}, u32[]{:S(2)}, u32[]{:S(2)}) collective-permute-start(bf16[360,128]{1,0:T(8,128)(2,1)S(1)} %get-tuple-element.83.refs_1_), channel_id=1, source_target_pairs={{0,24},{4,28},{8,16},{12,20},{16,8},{20,12},{24,0},{28,4},{1,25},{... | collective-permute-start | bytes 276488 | tf_op jit(solution)/shard_map/ppermute | solution.py:346
  71.0 24.3 %collective-permute-start.6 = (bf16[360,128]{1,0:T(8,128)(2,1)S(1)}, bf16[360,128]{1,0:T(8,128)(2,1)S(1)}, u32[]{:S(2)}, u32[]{:S(2)}) collective-permute-start(bf16[360,128]{1,0:T(8,128)(2,1)S(1)} %get-tuple-element.83.refs_1_), channel_id=1, source_target_pairs={{0,28},{4,24},{8,20},{12,16},{16,12},{20,8},{24,4},{28,0},{1,29},{... | collective-permute-start | bytes 276488 | tf_op jit(solution)/shard_map/ppermute | solution.py:346
  93.1 68.4 %collective-permute-start.29 = (bf16[4,640,128]{2,1,0:T(8,128)(2,1)}, bf16[4,640,128]{2,1,0:T(8,128)(2,1)S(1)}, u32[]{:S(2)}, u32[]{:S(2)}) collective-permute-start(bf16[4,640,128]{2,1,0:T(8,128)(2,1)} %get-tuple-element.63), channel_id=1, source_target_pairs={{0,4},{4,0},{8,12},{12,8},{16,20},{20,16},{24,28},{28,24},{1,5},{5... | collective-permute-start | bytes 1966088 | tf_op jit(solution)/shard_map/ppermute | solution.py:204
  94.2 73.8 %collective-permute-start.25 = (bf16[4,640,128]{2,1,0:T(8,128)(2,1)S(1)}, bf16[4,640,128]{2,1,0:T(8,128)(2,1)S(1)}, u32[]{:S(2)}, u32[]{:S(2)}) collective-permute-start(bf16[4,640,128]{2,1,0:T(8,128)(2,1)S(1)} %copy-done.64), channel_id=1, source_target_pairs={{0,4},{4,0},{8,12},{12,8},{16,20},{20,16},{24,28},{28,24},{1,5},{5... | collective-permute-start | bytes 1966088 | tf_op jit(solution)/shard_map/ppermute | solution.py:204
  159.5 17.9 %collective-permute-start.18 = (bf16[4,640,128]{2,1,0:T(8,128)(2,1)}, bf16[4,640,128]{2,1,0:T(8,128)(2,1)S(1)}, u32[]{:S(2)}, u32[]{:S(2)}) collective-permute-start(bf16[4,640,128]{2,1,0:T(8,128)(2,1)} %get-tuple-element.51), channel_id=1, source_target_pairs={{0,4},{4,0},{8,12},{12,8},{16,20},{20,16},{24,28},{28,24},{1,5},{5... | collective-permute-start | bytes 1966088 | tf_op jit(solution)/shard_map/ppermute | solution.py:204
  160.5 71.7 %collective-permute-start.14 = (bf16[4,896,128]{2,1,0:T(8,128)(2,1)}, bf16[4,896,128]{2,1,0:T(8,128)(2,1)S(1)}, u32[]{:S(2)}, u32[]{:S(2)}) collective-permute-start(bf16[4,896,128]{2,1,0:T(8,128)(2,1)} %get-tuple-element.44), channel_id=1, source_target_pairs={{0,4},{4,0},{8,12},{12,8},{16,20},{20,16},{24,28},{28,24},{1,5},{5... | collective-permute-start | bytes 2752520 | tf_op jit(solution)/shard_map/ppermute | solution.py:204
  165.5 11.9 %collective-permute-start.30 = (bf16[640,128]{1,0:T(8,128)(2,1)}, bf16[640,128]{1,0:T(8,128)(2,1)S(1)}, u32[]{:S(2)}, u32[]{:S(2)}) collective-permute-start(bf16[640,128]{1,0:T(8,128)(2,1)} %get-tuple-element.65), channel_id=1, source_target_pairs={{0,8},{4,12},{8,0},{12,4},{16,24},{20,28},{24,16},{28,20},{1,9},{5... | collective-permute-start | bytes 491528 | tf_op jit(solution)/shard_map/ppermute | solution.py:210
  165.5 17.4 %collective-permute-start.31 = (bf16[640,128]{1,0:T(8,128)(2,1)}, bf16[640,128]{1,0:T(8,128)(2,1)S(1)}, u32[]{:S(2)}, u32[]{:S(2)}) collective-permute-start(bf16[640,128]{1,0:T(8,128)(2,1)} %get-tuple-element.66), channel_id=1, source_target_pairs={{0,16},{4,20},{8,24},{12,28},{16,0},{20,4},{24,8},{28,12},{1,17},{... | collective-permute-start | bytes 491528 | tf_op jit(solution)/shard_map/ppermute | solution.py:210
  167.9 17.0 %collective-permute-start.32 = (bf16[640,128]{1,0:T(8,128)(2,1)}, bf16[640,128]{1,0:T(8,128)(2,1)S(1)}, u32[]{:S(2)}, u32[]{:S(2)}) collective-permute-start(bf16[640,128]{1,0:T(8,128)(2,1)} %get-tuple-element.67), channel_id=1, source_target_pairs={{0,24},{4,28},{8,16},{12,20},{16,8},{20,12},{24,0},{28,4},{1,25},{... | collective-permute-start | bytes 491528 | tf_op jit(solution)/shard_map/ppermute | solution.py:210
  177.4 10.6 %collective-permute-start.26 = (bf16[640,128]{1,0:T(8,128)(2,1)}, bf16[640,128]{1,0:T(8,128)(2,1)S(1)}, u32[]{:S(2)}, u32[]{:S(2)}) collective-permute-start(bf16[640,128]{1,0:T(8,128)(2,1)} %get-tuple-element.59), channel_id=1, source_target_pairs={{0,8},{4,12},{8,0},{12,4},{16,24},{20,28},{24,16},{28,20},{1,9},{5... | collective-permute-start | bytes 491528 | tf_op jit(solution)/shard_map/ppermute | solution.py:210
  177.4 20.6 %collective-permute-start.27 = (bf16[640,128]{1,0:T(8,128)(2,1)}, bf16[640,128]{1,0:T(8,128)(2,1)S(1)}, u32[]{:S(2)}, u32[]{:S(2)}) collective-permute-start(bf16[640,128]{1,0:T(8,128)(2,1)} %get-tuple-element.60), channel_id=1, source_target_pairs={{0,16},{4,20},{8,24},{12,28},{16,0},{20,4},{24,8},{28,12},{1,17},{... | collective-permute-start | bytes 491528 | tf_op jit(solution)/shard_map/ppermute | solution.py:210
  182.9 17.5 %collective-permute-start.28 = (bf16[640,128]{1,0:T(8,128)(2,1)}, bf16[640,128]{1,0:T(8,128)(2,1)S(1)}, u32[]{:S(2)}, u32[]{:S(2)}) collective-permute-start(bf16[640,128]{1,0:T(8,128)(2,1)} %get-tuple-element.61), channel_id=1, source_target_pairs={{0,24},{4,28},{8,16},{12,20},{16,8},{20,12},{24,0},{28,4},{1,25},{... | collective-permute-start | bytes 491528 | tf_op jit(solution)/shard_map/ppermute | solution.py:210
  185.0 43.7 %collective-permute-start.19 = (bf16[640,128]{1,0:T(8,128)(2,1)}, bf16[640,128]{1,0:T(8,128)(2,1)S(1)}, u32[]{:S(2)}, u32[]{:S(2)}) collective-permute-start(bf16[640,128]{1,0:T(8,128)(2,1)} %get-tuple-element.53), channel_id=1, source_target_pairs={{0,8},{4,12},{8,0},{12,4},{16,24},{20,28},{24,16},{28,20},{1,9},{5... | collective-permute-start | bytes 491528 | tf_op jit(solution)/shard_map/ppermute | solution.py:210
  188.0 41.5 %collective-permute-start.20 = (bf16[640,128]{1,0:T(8,128)(2,1)}, bf16[640,128]{1,0:T(8,128)(2,1)S(1)}, u32[]{:S(2)}, u32[]{:S(2)}) collective-permute-start(bf16[640,128]{1,0:T(8,128)(2,1)} %get-tuple-element.54), channel_id=1, source_target_pairs={{0,16},{4,20},{8,24},{12,28},{16,0},{20,4},{24,8},{28,12},{1,17},{... | collective-permute-start | bytes 491528 | tf_op jit(solution)/shard_map/ppermute | solution.py:210
  198.0 33.4 %collective-permute-start.21 = (bf16[640,128]{1,0:T(8,128)(2,1)}, bf16[640,128]{1,0:T(8,128)(2,1)S(1)}, u32[]{:S(2)}, u32[]{:S(2)}) collective-permute-start(bf16[640,128]{1,0:T(8,128)(2,1)} %get-tuple-element.55), channel_id=1, source_target_pairs={{0,24},{4,28},{8,16},{12,20},{16,8},{20,12},{24,0},{28,4},{1,25},{... | collective-permute-start | bytes 491528 | tf_op jit(solution)/shard_map/ppermute | solution.py:210
  217.0 3.8 collective-permute-start.37
  227.0 9.8 %collective-permute-start.40 = (bf16[640,128]{1,0:T(8,128)(2,1)}, bf16[640,128]{1,0:T(8,128)(2,1)S(1)}, u32[]{:S(2)}, u32[]{:S(2)}) collective-permute-start(bf16[640,128]{1,0:T(8,128)(2,1)} %get-tuple-element.72.refs_13_.refs_0_), channel_id=1, source_target_pairs={{0,8},{4,12},{8,0},{12,4},{16,24},{20,28},{24,16},{28,20},{1,9},{5... | collective-permute-start | bytes 491528 | tf_op jit(solution)/shard_map/ppermute | solution.py:281
  228.7 15.3 %collective-permute-start.42 = (bf16[640,128]{1,0:T(8,128)(2,1)}, bf16[640,128]{1,0:T(8,128)(2,1)S(1)}, u32[]{:S(2)}, u32[]{:S(2)}) collective-permute-start(bf16[640,128]{1,0:T(8,128)(2,1)} %get-tuple-element.72.refs_13_.refs_0_), channel_id=1, source_target_pairs={{0,16},{4,20},{8,24},{12,28},{16,0},{20,4},{24,8},{28,12},{1,17},{... | collective-permute-start | bytes 491528 | tf_op jit(solution)/shard_map/ppermute | solution.py:281
  229.5 14.4 %collective-permute-start.44 = (bf16[640,128]{1,0:T(8,128)(2,1)}, bf16[640,128]{1,0:T(8,128)(2,1)S(1)}, u32[]{:S(2)}, u32[]{:S(2)}) collective-permute-start(bf16[640,128]{1,0:T(8,128)(2,1)} %get-tuple-element.72.refs_13_.refs_0_), channel_id=1, source_target_pairs={{0,24},{4,28},{8,16},{12,20},{16,8},{20,12},{24,0},{28,4},{1,25},{... | collective-permute-start | bytes 491528 | tf_op jit(solution)/shard_map/ppermute | solution.py:281
  231.4 24.1 %collective-permute-start.47 = (bf16[640,128]{1,0:T(8,128)(2,1)}, bf16[640,128]{1,0:T(8,128)(2,1)S(1)}, u32[]{:S(2)}, u32[]{:S(2)}) collective-permute-start(bf16[640,128]{1,0:T(8,128)(2,1)} %get-tuple-element.73.refs_21_.refs_8_), channel_id=1, source_target_pairs={{0,8},{4,12},{8,0},{12,4},{16,24},{20,28},{24,16},{28,20},{1,9},{5... | collective-permute-start | bytes 491528 | tf_op jit(solution)/shard_map/ppermute | solution.py:281
  232.2 33.2 %collective-permute-start.49 = (bf16[640,128]{1,0:T(8,128)(2,1)}, bf16[640,128]{1,0:T(8,128)(2,1)S(1)}, u32[]{:S(2)}, u32[]{:S(2)}) collective-permute-start(bf16[640,128]{1,0:T(8,128)(2,1)} %get-tuple-element.73.refs_21_.refs_8_), channel_id=1, source_target_pairs={{0,16},{4,20},{8,24},{12,28},{16,0},{20,4},{24,8},{28,12},{1,17},{... | collective-permute-start | bytes 491528 | tf_op jit(solution)/shard_map/ppermute | solution.py:281
  236.8 28.6 %collective-permute-start.51 = (bf16[640,128]{1,0:T(8,128)(2,1)}, bf16[640,128]{1,0:T(8,128)(2,1)S(1)}, u32[]{:S(2)}, u32[]{:S(2)}) collective-permute-start(bf16[640,128]{1,0:T(8,128)(2,1)} %get-tuple-element.73.refs_21_.refs_8_), channel_id=1, source_target_pairs={{0,24},{4,28},{8,16},{12,20},{16,8},{20,12},{24,0},{28,4},{1,25},{... | collective-permute-start | bytes 491528 | tf_op jit(solution)/shard_map/ppermute | solution.py:281
  243.9 28.5 %collective-permute-start.15 = (bf16[896,128]{1,0:T(8,128)(2,1)}, bf16[896,128]{1,0:T(8,128)(2,1)S(1)}, u32[]{:S(2)}, u32[]{:S(2)}) collective-permute-start(bf16[896,128]{1,0:T(8,128)(2,1)} %get-tuple-element.46), channel_id=1, source_target_pairs={{0,8},{4,12},{8,0},{12,4},{16,24},{20,28},{24,16},{28,20},{1,9},{5... | collective-permute-start | bytes 688136 | tf_op jit(solution)/shard_map/ppermute | solution.py:210
  244.0 32.3 %collective-permute-start.16 = (bf16[896,128]{1,0:T(8,128)(2,1)}, bf16[896,128]{1,0:T(8,128)(2,1)S(1)}, u32[]{:S(2)}, u32[]{:S(2)}) collective-permute-start(bf16[896,128]{1,0:T(8,128)(2,1)} %get-tuple-element.47), channel_id=1, source_target_pairs={{0,16},{4,20},{8,24},{12,28},{16,0},{20,4},{24,8},{28,12},{1,17},{... | collective-permute-start | bytes 688136 | tf_op jit(solution)/shard_map/ppermute | solution.py:210
  255.5 14.9 %collective-permute-start.39 = (bf16[640,128]{1,0:T(8,128)(2,1)}, bf16[640,128]{1,0:T(8,128)(2,1)S(1)}, u32[]{:S(2)}, u32[]{:S(2)}) collective-permute-start(bf16[640,128]{1,0:T(8,128)(2,1)} %get-tuple-element.72.refs_13_.refs_0_), channel_id=1, source_target_pairs={{0,4},{4,0},{8,12},{12,8},{16,20},{20,16},{24,28},{28,24},{1,5},{5... | collective-permute-start | bytes 491528 | tf_op jit(solution)/shard_map/ppermute | solution.py:284
  265.4 5.5 %collective-permute-start.46 = (bf16[640,128]{1,0:T(8,128)(2,1)}, bf16[640,128]{1,0:T(8,128)(2,1)S(1)}, u32[]{:S(2)}, u32[]{:S(2)}) collective-permute-start(bf16[640,128]{1,0:T(8,128)(2,1)} %get-tuple-element.73.refs_21_.refs_8_), channel_id=1, source_target_pairs={{0,4},{4,0},{8,12},{12,8},{16,20},{20,16},{24,28},{28,24},{1,5},{5... | collective-permute-start | bytes 491528 | tf_op jit(solution)/shard_map/ppermute | solution.py:284
  265.4 12.9 %collective-permute-start.17 = (bf16[896,128]{1,0:T(8,128)(2,1)}, bf16[896,128]{1,0:T(8,128)(2,1)S(1)}, u32[]{:S(2)}, u32[]{:S(2)}) collective-permute-start(bf16[896,128]{1,0:T(8,128)(2,1)} %get-tuple-element.48), channel_id=1, source_target_pairs={{0,24},{4,28},{8,16},{12,20},{16,8},{20,12},{24,0},{28,4},{1,25},{... | collective-permute-start | bytes 688136 | tf_op jit(solution)/shard_map/ppermute | solution.py:210
  270.4 8.0 %collective-permute-start.41 = (bf16[640,128]{1,0:T(8,128)(2,1)S(1)}, bf16[640,128]{1,0:T(8,128)(2,1)S(1)}, u32[]{:S(2)}, u32[]{:S(2)}) collective-permute-start(bf16[640,128]{1,0:T(8,128)(2,1)S(1)} %collective-permute-done.40.refs_15_.refs_2_), channel_id=1, source_target_pairs={{0,4},{4,0},{8,12},{12,8},{16,20},{20,16},{24,28},{28,24},{1,5},{5... | collective-permute-start | bytes 491528 | tf_op jit(solution)/shard_map/ppermute | solution.py:284
  270.9 12.0 %collective-permute-start.43 = (bf16[640,128]{1,0:T(8,128)(2,1)S(1)}, bf16[640,128]{1,0:T(8,128)(2,1)S(1)}, u32[]{:S(2)}, u32[]{:S(2)}) collective-permute-start(bf16[640,128]{1,0:T(8,128)(2,1)S(1)} %collective-permute-done.42.refs_17_.refs_4_), channel_id=1, source_target_pairs={{0,4},{4,0},{8,12},{12,8},{16,20},{20,16},{24,28},{28,24},{1,5},{5... | collective-permute-start | bytes 491528 | tf_op jit(solution)/shard_map/ppermute | solution.py:284
  272.4 10.5 %collective-permute-start.45 = (bf16[640,128]{1,0:T(8,128)(2,1)S(1)}, bf16[640,128]{1,0:T(8,128)(2,1)S(1)}, u32[]{:S(2)}, u32[]{:S(2)}) collective-permute-start(bf16[640,128]{1,0:T(8,128)(2,1)S(1)} %collective-permute-done.44.refs_19_.refs_6_), channel_id=1, source_target_pairs={{0,4},{4,0},{8,12},{12,8},{16,20},{20,16},{24,28},{28,24},{1,5},{5... | collective-permute-start | bytes 491528 | tf_op jit(solution)/shard_map/ppermute | solution.py:284
  276.3 8.8 %collective-permute-start.48 = (bf16[640,128]{1,0:T(8,128)(2,1)S(1)}, bf16[640,128]{1,0:T(8,128)(2,1)S(1)}, u32[]{:S(2)}, u32[]{:S(2)}) collective-permute-start(bf16[640,128]{1,0:T(8,128)(2,1)S(1)} %collective-permute-done.47.refs_23_.refs_10_), channel_id=1, source_target_pairs={{0,4},{4,0},{8,12},{12,8},{16,20},{20,16},{24,28},{28,24},{1,5},{5... | collective-permute-start | bytes 491528 | tf_op jit(solution)/shard_map/ppermute | solution.py:284
  278.3 9.7 %collective-permute-start.50 = (bf16[640,128]{1,0:T(8,128)(2,1)S(1)}, bf16[640,128]{1,0:T(8,128)(2,1)S(1)}, u32[]{:S(2)}, u32[]{:S(2)}) collective-permute-start(bf16[640,128]{1,0:T(8,128)(2,1)S(1)} %collective-permute-done.49.refs_25_.refs_12_), channel_id=1, source_target_pairs={{0,4},{4,0},{8,12},{12,8},{16,20},{20,16},{24,28},{28,24},{1,5},{5... | collective-permute-start | bytes 491528 | tf_op jit(solution)/shard_map/ppermute | solution.py:284
  278.4 11.4 %collective-permute-start.52 = (bf16[640,128]{1,0:T(8,128)(2,1)S(1)}, bf16[640,128]{1,0:T(8,128)(2,1)S(1)}, u32[]{:S(2)}, u32[]{:S(2)}) collective-permute-start(bf16[640,128]{1,0:T(8,128)(2,1)S(1)} %collective-permute-done.51.refs_27_.refs_14_), channel_id=1, source_target_pairs={{0,4},{4,0},{8,12},{12,8},{16,20},{20,16},{24,28},{28,24},{1,5},{5... | collective-permute-start | bytes 491528 | tf_op jit(solution)/shard_map/ppermute | solution.py:284
  282.9 6.8 %collective-permute-start.22 = (f32[256,128]{1,0:T(8,128)}, f32[256,128]{1,0:T(8,128)S(1)}, u32[]{:S(2)}, u32[]{:S(2)}) collective-permute-start(f32[256,128]{1,0:T(8,128)} %gram.1.refs_9_), channel_id=1, source_target_pairs={{0,1},{1,0},{2,3},{3,2},{4,5},{5,4},{6,7},{7,6},{8,9},{9,8},{10,11... | collective-permute-start | bytes 393224 | tf_op jit(solution)/shard_map/ppermute | solution.py:215
  283.0 6.8 %collective-permute-start.23 = (f32[256,128]{1,0:T(8,128)}, f32[256,128]{1,0:T(8,128)S(1)}, u32[]{:S(2)}, u32[]{:S(2)}) collective-permute-start(f32[256,128]{1,0:T(8,128)} %gram.1.refs_9_), channel_id=1, source_target_pairs={{0,2},{1,3},{2,0},{3,1},{4,6},{5,7},{6,4},{7,5},{8,10},{9,11},{10,... | collective-permute-start | bytes 393224 | tf_op jit(solution)/shard_map/ppermute | solution.py:215
  285.1 6.3 %collective-permute-start.24 = (f32[256,128]{1,0:T(8,128)}, f32[256,128]{1,0:T(8,128)S(1)}, u32[]{:S(2)}, u32[]{:S(2)}) collective-permute-start(f32[256,128]{1,0:T(8,128)} %gram.1.refs_9_), channel_id=1, source_target_pairs={{0,3},{1,2},{2,1},{3,0},{4,7},{5,6},{6,5},{7,4},{8,11},{9,10},{10,... | collective-permute-start | bytes 393224 | tf_op jit(solution)/shard_map/ppermute | solution.py:215
  298.1 3.7 collective-permute-start.54
  306.0 3.8 collective-permute-start.57
  312.9 12.2 %collective-permute-start.67 = (bf16[640,128]{1,0:T(8,128)(2,1)}, bf16[640,128]{1,0:T(8,128)(2,1)S(1)}, u32[]{:S(2)}, u32[]{:S(2)}) collective-permute-start(bf16[640,128]{1,0:T(8,128)(2,1)} %get-tuple-element.79.refs_0_), channel_id=1, source_target_pairs={{0,8},{4,12},{8,0},{12,4},{16,24},{20,28},{24,16},{28,20},{1,9},{5... | collective-permute-start | bytes 491528 | tf_op jit(solution)/shard_map/ppermute | solution.py:281
  315.8 15.3 %collective-permute-start.69 = (bf16[640,128]{1,0:T(8,128)(2,1)}, bf16[640,128]{1,0:T(8,128)(2,1)S(1)}, u32[]{:S(2)}, u32[]{:S(2)}) collective-permute-start(bf16[640,128]{1,0:T(8,128)(2,1)} %get-tuple-element.79.refs_0_), channel_id=1, source_target_pairs={{0,16},{4,20},{8,24},{12,28},{16,0},{20,4},{24,8},{28,12},{1,17},{... | collective-permute-start | bytes 491528 | tf_op jit(solution)/shard_map/ppermute | solution.py:281
  317.0 16.7 %collective-permute-start.71 = (bf16[640,128]{1,0:T(8,128)(2,1)}, bf16[640,128]{1,0:T(8,128)(2,1)S(1)}, u32[]{:S(2)}, u32[]{:S(2)}) collective-permute-start(bf16[640,128]{1,0:T(8,128)(2,1)} %get-tuple-element.79.refs_0_), channel_id=1, source_target_pairs={{0,24},{4,28},{8,16},{12,20},{16,8},{20,12},{24,0},{28,4},{1,25},{... | collective-permute-start | bytes 491528 | tf_op jit(solution)/shard_map/ppermute | solution.py:281
  318.5 17.2 %collective-permute-start.66 = (bf16[640,128]{1,0:T(8,128)(2,1)}, bf16[640,128]{1,0:T(8,128)(2,1)S(1)}, u32[]{:S(2)}, u32[]{:S(2)}) collective-permute-start(bf16[640,128]{1,0:T(8,128)(2,1)} %get-tuple-element.79.refs_0_), channel_id=1, source_target_pairs={{0,4},{4,0},{8,12},{12,8},{16,20},{20,16},{24,28},{28,24},{1,5},{5... | collective-permute-start | bytes 491528 | tf_op jit(solution)/shard_map/ppermute | solution.py:284
  320.5 15.3 %collective-permute-start.60 = (bf16[640,128]{1,0:T(8,128)(2,1)}, bf16[640,128]{1,0:T(8,128)(2,1)S(1)}, u32[]{:S(2)}, u32[]{:S(2)}) collective-permute-start(bf16[640,128]{1,0:T(8,128)(2,1)} %get-tuple-element.78.refs_0_), channel_id=1, source_target_pairs={{0,8},{4,12},{8,0},{12,4},{16,24},{20,28},{24,16},{28,20},{1,9},{5... | collective-permute-start | bytes 491528 | tf_op jit(solution)/shard_map/ppermute | solution.py:281
  325.1 84.8 %collective-permute-start.62 = (bf16[640,128]{1,0:T(8,128)(2,1)}, bf16[640,128]{1,0:T(8,128)(2,1)S(1)}, u32[]{:S(2)}, u32[]{:S(2)}) collective-permute-start(bf16[640,128]{1,0:T(8,128)(2,1)} %get-tuple-element.78.refs_0_), channel_id=1, source_target_pairs={{0,16},{4,20},{8,24},{12,28},{16,0},{20,4},{24,8},{28,12},{1,17},{... | collective-permute-start | bytes 491528 | tf_op jit(solution)/shard_map/ppermute | solution.py:281
  331.0 78.9 %collective-permute-start.64 = (bf16[640,128]{1,0:T(8,128)(2,1)}, bf16[640,128]{1,0:T(8,128)(2,1)S(1)}, u32[]{:S(2)}, u32[]{:S(2)}) collective-permute-start(bf16[640,128]{1,0:T(8,128)(2,1)} %get-tuple-element.78.refs_0_), channel_id=1, source_target_pairs={{0,24},{4,28},{8,16},{12,20},{16,8},{20,12},{24,0},{28,4},{1,25},{... | collective-permute-start | bytes 491528 | tf_op jit(solution)/shard_map/ppermute | solution.py:281
  333.8 78.2 %collective-permute-start.68 = (bf16[640,128]{1,0:T(8,128)(2,1)S(1)}, bf16[640,128]{1,0:T(8,128)(2,1)S(1)}, u32[]{:S(2)}, u32[]{:S(2)}) collective-permute-start(bf16[640,128]{1,0:T(8,128)(2,1)S(1)} %collective-permute-done.67.refs_2_), channel_id=1, source_target_pairs={{0,4},{4,0},{8,12},{12,8},{16,20},{20,16},{24,28},{28,24},{1,5},{5... | collective-permute-start | bytes 491528 | tf_op jit(solution)/shard_map/ppermute | solution.py:284
  335.7 76.4 %collective-permute-start.70 = (bf16[640,128]{1,0:T(8,128)(2,1)S(1)}, bf16[640,128]{1,0:T(8,128)(2,1)S(1)}, u32[]{:S(2)}, u32[]{:S(2)}) collective-permute-start(bf16[640,128]{1,0:T(8,128)(2,1)S(1)} %collective-permute-done.69.refs_4_), channel_id=1, source_target_pairs={{0,4},{4,0},{8,12},{12,8},{16,20},{20,16},{24,28},{28,24},{1,5},{5... | collective-permute-start | bytes 491528 | tf_op jit(solution)/shard_map/ppermute | solution.py:284
  335.8 78.2 %collective-permute-start.72 = (bf16[640,128]{1,0:T(8,128)(2,1)S(1)}, bf16[640,128]{1,0:T(8,128)(2,1)S(1)}, u32[]{:S(2)}, u32[]{:S(2)}) collective-permute-start(bf16[640,128]{1,0:T(8,128)(2,1)S(1)} %collective-permute-done.71.refs_6_), channel_id=1, source_target_pairs={{0,4},{4,0},{8,12},{12,8},{16,20},{20,16},{24,28},{28,24},{1,5},{5... | collective-permute-start | bytes 491528 | tf_op jit(solution)/shard_map/ppermute | solution.py:284
  409.9 34.8 %collective-permute-start.59 = (bf16[640,128]{1,0:T(8,128)(2,1)S(1)}, bf16[640,128]{1,0:T(8,128)(2,1)S(1)}, u32[]{:S(2)}, u32[]{:S(2)}) collective-permute-start(bf16[640,128]{1,0:T(8,128)(2,1)S(1)} %copy-done.23), channel_id=1, source_target_pairs={{0,4},{4,0},{8,12},{12,8},{16,20},{20,16},{24,28},{28,24},{1,5},{5... | collective-permute-start | bytes 491528 | tf_op jit(solution)/shard_map/ppermute | solution.py:284
  409.9 34.8 %collective-permute-start.61 = (bf16[640,128]{1,0:T(8,128)(2,1)S(1)}, bf16[640,128]{1,0:T(8,128)(2,1)S(1)}, u32[]{:S(2)}, u32[]{:S(2)}) collective-permute-start(bf16[640,128]{1,0:T(8,128)(2,1)S(1)} %collective-permute-done.60.refs_2_), channel_id=1, source_target_pairs={{0,4},{4,0},{8,12},{12,8},{16,20},{20,16},{24,28},{28,24},{1,5},{5... | collective-permute-start | bytes 491528 | tf_op jit(solution)/shard_map/ppermute | solution.py:284
  412.0 32.8 %collective-permute-start.63 = (bf16[640,128]{1,0:T(8,128)(2,1)S(1)}, bf16[640,128]{1,0:T(8,128)(2,1)S(1)}, u32[]{:S(2)}, u32[]{:S(2)}) collective-permute-start(bf16[640,128]{1,0:T(8,128)(2,1)S(1)} %collective-permute-done.62.refs_4_), channel_id=1, source_target_pairs={{0,4},{4,0},{8,12},{12,8},{16,20},{20,16},{24,28},{28,24},{1,5},{5... | collective-permute-start | bytes 491528 | tf_op jit(solution)/shard_map/ppermute | solution.py:284
  412.1 32.7 %collective-permute-start.65 = (bf16[640,128]{1,0:T(8,128)(2,1)S(1)}, bf16[640,128]{1,0:T(8,128)(2,1)S(1)}, u32[]{:S(2)}, u32[]{:S(2)}) collective-permute-start(bf16[640,128]{1,0:T(8,128)(2,1)S(1)} %collective-permute-done.64.refs_6_), channel_id=1, source_target_pairs={{0,4},{4,0},{8,12},{12,8},{16,20},{20,16},{24,28},{28,24},{1,5},{5... | collective-permute-start | bytes 491528 | tf_op jit(solution)/shard_map/ppermute | solution.py:284
  (88 other events, 1545.6 us)
